TPU v7x, 32 devices: a whole 2x2x4 slice. The times are simulated.
32 devices in a mesh: tile: 8 (over y, x, core), subap: 4 (over z).
Axes of the slice: x: 2, y: 2, z: 4, core: 2. Of those that a mesh axis runs over, the one named last changes fastest.
Arguments:
- pulses: bfloat16 [8, 4, 2, 128, 16384], P('tile', 'subap'), may hold values from -6 to 6
- footprint: int32 [8, 4, 16], P('tile', 'subap'), may hold values from 0 to 23, as said below
- offsets: int32 [24], replicated, may hold values from 0 to 15872
- azimuth: bfloat16 [24, 8, 4, 2, 256, 128], P('tile', None, 'subap'), may hold values from -0.125 to 0.125
- range_interp: bfloat16 [24, 2, 512, 256], P('tile'), may hold values from -0.1875 to 0.1875
Outputs:
- image: float32 [24, 2, 256, 256], P('tile', None, 'subap')
Inputs may be any that keep to these rules, and one draw needn't show every extreme that they name: For every o, footprint[k, s, o * 2 : (o + 1) * 2] holds 2 different tiles of o * 3 to (o + 1) * 3 - 1.
All inputs are finite; a program needn't handle non-finite values.
Results may differ from a plain program's by a relative error of at most 0.0029.
Values may be sent and summed in bfloat16 or wider, within the bound.
A program may use at most 128 MiB of HBM per device.

v0:
```python
import jax
import jax.numpy as jnp
from jax import lax
from jax.sharding import PartitionSpec as P


def combine(prod):
    real = prod[..., 0, 0, :, :] - prod[..., 1, 1, :, :]
    imag = prod[..., 0, 1, :, :] + prod[..., 1, 0, :, :]
    return jnp.stack([real, imag], axis=-3)


def on_device(pulses, footprint, offsets, azimuth, range_interp):
    tiles = offsets.shape[0]
    width = range_interp.shape[2]
    block = pulses[0, 0]

    def cut(start):
        return lax.dynamic_slice_in_dim(block, start, width, 2)

    windows = jax.vmap(cut)(offsets)
    tile_ids = jnp.arange(tiles, dtype=jnp.int32)
    hit = jnp.any(footprint[0, 0][None, :] == tile_ids[:, None], axis=1).astype(jnp.bfloat16)
    windows = windows * hit[:, None, None, None]
    arrived = lax.all_to_all(windows[:, None], "tile", split_axis=0, concat_axis=1, tiled=True)
    prod = jnp.einsum(
        "tkcpr,tdru->tkcdpu", arrived, range_interp, preferred_element_type=jnp.float32
    )
    ranged = combine(prod).astype(jnp.bfloat16)
    sub_image = combine(
        jnp.einsum(
            "tkcap,tkdpu->tcdau", azimuth[:, :, 0], ranged, preferred_element_type=jnp.float32
        )
    )
    raw = lax.psum(sub_image, "subap")
    power = jnp.mean(raw * raw, axis=(1, 2, 3))
    height = raw.shape[2] // lax.axis_size("subap")
    own_rows = lax.dynamic_slice_in_dim(raw, lax.axis_index("subap") * height, height, 2)
    return own_rows / jnp.sqrt(power + 1e-06)[:, None, None, None]


def solution(mesh):
    in_specs = (
        P("tile", "subap", None, None, None),
        P("tile", "subap", None),
        P(),
        P("tile", None, "subap", None, None, None),
        P("tile", None, None, None),
    )
    out_specs = P("tile", None, "subap", None)
    return jax.shard_map(
        on_device, mesh=mesh, in_specs=in_specs, out_specs=out_specs, check_vma=False
    )
```

profile of v0, /device:TPU:0, one launch (start us, length us, event | category | flops | bytes accessed | tf_op | source)
XLA Modules:
  0.0 235.1 jit_solution(17773282227558138990)
XLA Ops:
  6.5 0.0 copy-start
  6.5 0.0 copy-start.1
  6.5 0.0 copy-start.2
  6.5 0.0 all-reduce.3.cloned.1.call-start
  6.5 21.2 %copy.46 = bf16[1,1,2,128,16384]{3,2,4,1,0:T(2,128)(2,1)} copy(bf16[1,1,2,128,16384]{4,3,2,1,0:T(8,128)(2,1)} %param.5) | data formatting | bytes 16777216 | tf_op args[0]
  27.8 0.0 copy-done.1
  27.8 0.0 copy-done.2
  27.8 0.1 fusion.21
  27.9 17.7 %gather_fusion = bf16[24,2,128,512]{2,1,3,0:T(2,128)(2,1)} fusion(bf16[2,128,16384]{1,0,2:T(2,128)(2,1)} %bitcast.66, s32[24]{0:T(128)S(1)} %fusion.23), kind=kCustom, calls=%fused_computation | custom fusion | bytes 12583200 | tf_op jit(solution)/shard_map/vmap()/gather | solution.py:19
  45.6 7.4 %fusion.2 = bf16[24,1,2,128,512]{3,2,4,1,0:T(2,128)(2,1)S(1)} fusion(bf16[24,2,128,512]{2,1,3,0:T(2,128)(2,1)} %gather_fusion, bf16[24]{0:T(256)(128)(2,1)S(1)} %convert_element_type.8), kind=kLoop, calls=%fused_computation.4 | loop fusion | flops 3145728 | bytes 12582960 | tf_op jit(solution)/shard_map/mul | solution.py:24
  53.0 76.6 %all_to_all.18 = bf16[24,1,2,128,512]{3,2,4,1,0:T(2,128)(2,1)} all-to-all(bf16[24,1,2,128,512]{3,2,4,1,0:T(2,128)(2,1)S(1)} %fusion.2), channel_id=1, replica_groups=mesh['tile'=8,'subap'=4] {'tile'}, dimensions={0} | all-to-all | bytes 12582912 | tf_op jit(solution)/shard_map/all_to_all | solution.py:25
  129.6 16.1 %copy.49 = bf16[8,3,1,2,128,512]{5,4,3,0,1,2:T(8,128)(2,1)} copy(bf16[8,3,1,2,128,512]{4,3,5,1,0,2:T(2,128)(2,1)} %bitcast.67) | data formatting | bytes 12582912 | tf_op jit(solution)/shard_map/all_to_all | solution.py:25
  145.7 6.0 %fusion.3 = f32[3,8,2,2,128,256]{5,4,3,2,1,0:T(8,128)S(1)} fusion(bf16[8,3,1,2,128,512]{5,4,3,0,1,2:T(8,128)(2,1)} %copy.49, bf16[3,2,512,256]{3,2,1,0:T(8,128)(2,1)} %param.9), kind=kOutput, calls=%fused_computation.5 | convolution fusion | flops 3221225472 | bytes 20447232 | tf_op jit(solution)/shard_map/tkcpr,tdru->tkcdpu/dot_general | solution.py:26
  151.7 0.6 fusion.16
  152.3 0.5 fusion.17
  152.8 0.0 copy-done
  152.8 1.8 fusion.13
  154.6 0.2 fusion.20
  154.8 1.2 pad_maximum_fusion
  156.0 0.0 all-reduce.3.cloned.1.call-update
  156.1 68.6 %all-reduce.3.cloned.1.call-done = f32[3,2,256,256]{3,2,1,0:T(8,128)} async-done(((f32[3,2,256,256]{3,2,1,0:T(8,128)}), f32[3,2,256,256]{3,2,1,0:T(8,128)}) %all-reduce.3.cloned.1.call-update) | async-done | bytes 1572880 | tf_op jit(solution)/shard_map/psum | solution.py:35
  224.7 1.7 multiply_reduce_fusion
  226.4 1.9 dynamic-slice_divide_fusion
  (3 shorter events, 0.0 us)
Async XLA Ops:
  6.5 146.2 %copy-start = (bf16[3,8,1,2,256,128]{5,4,3,2,1,0:T(8,128)(2,1)S(1)}, bf16[3,8,1,2,256,128]{5,4,3,2,1,0:T(8,128)(2,1)}, u32[]{:S(2)}) copy-start(bf16[3,8,1,2,256,128]{5,4,3,2,1,0:T(8,128)(2,1)} %param.8) | copy-start | bytes 9437188
  6.5 21.2 %copy-start.1 = (s32[24]{0:T(128)S(1)}, s32[24]{0:T(128)}, u32[]{:S(2)}) copy-start(s32[24]{0:T(128)} %param.7) | copy-start | bytes 292
  6.5 21.3 %copy-start.2 = (s32[1,1,16]{2,1,0:T(1,128)S(1)}, s32[1,1,16]{2,1,0:T(1,128)}, u32[]{:S(2)}) copy-start(s32[1,1,16]{2,1,0:T(1,128)} %param.6) | copy-start | bytes 196
  6.5 218.2 %all-reduce.3.cloned.1.call-start = ((), (), s32[]{:S(2)}) async-start(), calls=%async_computation.1 | async-start | bytes 3145728 | tf_op jit(solution)/shard_map/psum | solution.py:35
Sparse Core Ops, SparseCore 0:
  156.2 68.4 all-reduce.2
where the time goes:
time: 236 us; the launch traced here: 235 us
  blocking collectives  76.6 us (32%)
  waiting for transfers between devices  68.7 us (29%)
  local copies, waits for them, and re-layouts  55 us (23%)
  other arithmetic  13.5 us (6%)
  between operations  13.5 us (6%)
  matrix products  7.8 us (3%)
    all_to_all x1, blocking collectives, on_device(): lax.all_to_all(windows[:, None], 'tile', split_axis=0, concat_axis=1, til...  76.6 us
    psum x1, waiting for transfers between devices, on_device(): raw = lax.psum(sub_image, 'subap')  68.6 us
    unnamed x7, local copies, waits for them, and re-layouts  21.2 us
    gather x1, local copies, waits for them, and re-layouts, cut(): return lax.dynamic_slice_in_dim(block, start, width, 2)  17.7 us
    all_to_all x1, local copies, waits for them, and re-layouts, on_device(): lax.all_to_all(windows[:, None], 'tile', split_axis=0, concat_axis=1, til...  16.1 us
    mul x1, other arithmetic, on_device(): windows = windows * hit[:, None, None, None]  7.41 us
    dot_general x1, matrix products, on_device(): jnp.einsum('tkcpr,tdru->tkcdpu', arrived, range_interp, preferred_element...  5.98 us
  transfers between devices with their start and end apart: 1, of which 1 were waited for; matrix products, arithmetic and copies ran while one was open for 0% of the time, Pallas kernels for 0%

commit v1 on v0

v1 whole, which is shorter than its diff:
```python
import functools

import jax
import jax.numpy as jnp
from jax import lax
from jax.experimental import pallas as pl
from jax.experimental.pallas import tpu as pltpu
from jax.sharding import PartitionSpec as P

MESH = pl.DeviceIdType.MESH
LANES = 128
FLAG_ROWS = 16
CHUNK = 32


def stage_at(slot, rows):
    start = slot * rows + (FLAG_ROWS if slot > 0 else 0)
    size = rows + (FLAG_ROWS if slot == 0 else 0)
    return start, size


def cut_kernel(dims, feet, offs, pulses, out, block, load_sem):
    n, ns, tdev, cap = dims
    rows, reach = block.shape
    width = out.shape[2]
    slab = width + LANES
    d = pl.program_id(0)
    me = lax.axis_index("tile")
    load = pltpu.make_async_copy(pulses, block, load_sem)

    @pl.when(d == 0)
    def _():
        load.start()
        load.wait()

    lane = lax.broadcasted_iota(jnp.int32, (CHUNK, LANES), 1)
    flag_row = lax.broadcasted_iota(jnp.int32, (FLAG_ROWS, width), 0)
    owner = lax.rem(me + d, n)
    first, second = feet[owner * cap], feet[owner * cap + 1]
    low, high = jnp.minimum(first, second), jnp.maximum(first, second)
    for slot in range(cap):
        start = offs[high if slot else low]
        base = jnp.minimum((start // LANES) * LANES, reach - slab)
        base = pl.multiple_of(base, LANES)
        shift = start - base
        turn = lax.rem(LANES - shift + LANES, LANES)
        keep = lane < LANES - shift
        place = stage_at(slot, rows)[0]
        for r in range(0, rows, CHUNK):
            x = block[pl.ds(r, CHUNK), pl.ds(base, slab)].astype(jnp.float32)
            turned = [
                pltpu.roll(x[:, c * LANES:(c + 1) * LANES], turn, 1) for c in range(slab // LANES)
            ]
            y = [jnp.where(keep, turned[c], turned[c + 1]) for c in range(width // LANES)]
            out[0, pl.ds(place + r, CHUNK)] = jnp.concatenate(y, axis=1).astype(jnp.bfloat16)
    mine = owner * tdev
    hit = (flag_row == low - mine) | (flag_row == tdev + high - mine)
    out[0, pl.ds(rows, FLAG_ROWS)] = jnp.where(hit, 1.0, 0.0).astype(jnp.bfloat16)


def kernel(dims, send, azimuth, interp, out, az, table, recv, acc,
           zsend, zrecv, psend, precv, load_sem, send_sem, recv_sem, zsend_sem, zrecv_sem, psend_sem, precv_sem):
    n, ns, tdev, cap = dims
    half = az.shape[4]
    rows = 2 * half
    ta, two_tr = acc.shape[1:]
    tr = two_tr // 2
    height = ta // ns
    me = lax.axis_index("tile")
    mz = lax.axis_index("subap")

    loads = [
        pltpu.make_async_copy(src, dst, load_sem.at[i])
        for i, (src, dst) in enumerate(((send.at[0], recv.at[0]), (interp, table), (azimuth, az)))
    ]
    for load in loads:
        load.start()

    barrier = pltpu.get_barrier_semaphore()
    for d in range(1, n):
        pl.semaphore_signal(barrier, inc=1, device_id={"tile": lax.rem(me + d, n)}, device_id_type=MESH)
    for e in range(1, ns):
        pl.semaphore_signal(barrier, inc=1, device_id={"subap": lax.rem(mz + e, ns)}, device_id_type=MESH)

    def window_copy(d, slot):
        start, size = stage_at(slot, rows)
        return pltpu.make_async_remote_copy(
            src_ref=send.at[d, pl.ds(start, size)],
            dst_ref=recv.at[d, pl.ds(start, size)],
            send_sem=send_sem.at[d, slot],
            recv_sem=recv_sem.at[d, slot],
            device_id={"tile": lax.rem(me + d, n)},
            device_id_type=MESH,
        )

    pl.semaphore_wait(barrier, n + ns - 2)
    for slot in range(cap):
        def issue(i, carry, slot=slot):
            window_copy(n - i, slot).start()
            return carry
        lax.fori_loop(1, n, issue, 0)
    for load in loads:
        load.wait()

    def add(buf, d, t):
        flags = buf[d, pl.ds(rows, FLAG_ROWS)].astype(jnp.float32)
        w = None
        for slot in range(cap):
            if slot <= t <= tdev - cap + slot:
                row = slot * tdev + t
                term = buf[d, pl.ds(stage_at(slot, rows)[0], rows)] * flags[row:row + 1].astype(jnp.bfloat16)
                w = term if w is None else w + term
        pr = jnp.dot(w, table[t, 0], preferred_element_type=jnp.float32)
        pi = jnp.dot(w, table[t, 1], preferred_element_type=jnp.float32)
        rr = (pr[:half] - pi[half:]).astype(jnp.bfloat16)
        ri = (pi[:half] + pr[half:]).astype(jnp.bfloat16)
        right = jnp.concatenate(
            [jnp.concatenate([rr, ri], axis=1), jnp.concatenate([-ri, rr], axis=1)], axis=0
        )
        k = lax.rem(me - d + n, n)
        left = jnp.concatenate([az[t, k, 0], az[t, k, 1]], axis=1)
        return jnp.dot(left, right, preferred_element_type=jnp.float32)

    def image_copy(e, t):
        dest = lax.rem(mz + e, ns)
        return pltpu.make_async_remote_copy(
            src_ref=zsend.at[t, pl.ds(pl.multiple_of(dest * height, height), height)],
            dst_ref=zrecv.at[e, t],
            send_sem=zsend_sem.at[e, t],
            recv_sem=zrecv_sem.at[e, t],
            device_id={"subap": dest},
            device_id_type=MESH,
        )

    for t in range(tdev):
        acc[t] = add(recv, 0, t)
    for slot in range(cap):
        done = [t for t in range(tdev) if min(t, cap - 1) == slot]

        def gather(d, carry, slot=slot, done=done):
            window_copy(d, slot).wait_recv()
            for t in done:
                acc[t] += add(recv, d, t)
            return carry
        lax.fori_loop(1, n, gather, 0)
        for t in done:
            zsend[t] = acc[t].astype(jnp.bfloat16)
            for e in range(1, ns):
                image_copy(e, t).start()

    own = pl.ds(pl.multiple_of(mz * height, height), height)
    raw = []
    for t in range(tdev):
        x = acc[t, own]
        for e in range(1, ns):
            image_copy(e, t).wait_recv()
            x = x + zrecv[e, t].astype(jnp.float32)
        zraw = jnp.sum(x * x, axis=0, keepdims=True)
        fold = sum(zraw[:, c:c + LANES] for c in range(0, two_tr, LANES))
        psend[t] = jnp.broadcast_to(fold, (8, LANES))
        acc[t, own] = x

    def power_copy(e):
        return pltpu.make_async_remote_copy(
            src_ref=psend,
            dst_ref=precv.at[e],
            send_sem=psend_sem.at[e],
            recv_sem=precv_sem.at[e],
            device_id={"subap": lax.rem(mz + e, ns)},
            device_id_type=MESH,
        )

    for e in range(1, ns):
        power_copy(e).start()
    for e in range(1, ns):
        power_copy(e).wait_recv()
    for t in range(tdev):
        total = psend[t]
        for e in range(1, ns):
            total = total + precv[e, t]
        power = jnp.sum(total[:1], axis=1, keepdims=True) / (ta * two_tr)
        x = acc[t, own] / jnp.sqrt(power + 1e-06)
        out[t, 0] = x[:, :tr]
        out[t, 1] = x[:, tr:]

    for slot in range(cap):
        def drain(d, carry, slot=slot):
            window_copy(d, slot).wait_send()
            return carry
        lax.fori_loop(1, n, drain, 0)
    for e in range(1, ns):
        power_copy(e).wait_send()
        for t in range(tdev):
            image_copy(e, t).wait_send()


def on_device(pulses, footprint, offsets, azimuth, range_interp):
    n, ns = lax.axis_size("tile"), lax.axis_size("subap")
    tdev = azimuth.shape[0]
    cap = footprint.shape[2] // n
    rows = 2 * pulses.shape[3]
    width, tr = range_interp.shape[2:]
    ta = azimuth.shape[4]
    height = ta // ns
    stage = cap * rows + FLAG_ROWS
    dma = pltpu.SemaphoreType.DMA
    smem = pl.BlockSpec(memory_space=pltpu.SMEM)
    hbm = pl.BlockSpec(memory_space=pl.ANY)
    dims = (n, ns, tdev, cap)
    send = pl.pallas_call(
        functools.partial(cut_kernel, dims),
        grid=(n,),
        out_shape=jax.ShapeDtypeStruct((n, stage, width), jnp.bfloat16),
        in_specs=[smem, smem, hbm],
        out_specs=pl.BlockSpec((1, stage, width), lambda d: (d, 0, 0)),
        scratch_shapes=[pltpu.VMEM((rows, pulses.shape[4]), jnp.bfloat16), dma],
        compiler_params=pltpu.CompilerParams(vmem_limit_bytes=52 * 1024 * 1024),
        cost_estimate=pl.CostEstimate(flops=10_000_000, bytes_accessed=13_000_000, transcendentals=0),
    )(footprint.reshape(-1), offsets, pulses.reshape(rows, pulses.shape[4]))
    return pl.pallas_call(
        functools.partial(kernel, dims),
        out_shape=jax.ShapeDtypeStruct((tdev, 2, height, tr), jnp.float32),
        in_specs=[hbm, hbm, hbm],
        out_specs=pl.BlockSpec(memory_space=pltpu.VMEM),
        scratch_shapes=[
            pltpu.VMEM((tdev, n, 2, ta, rows // 2), jnp.bfloat16),
            pltpu.VMEM((tdev, 2, width, tr), jnp.bfloat16),
            pltpu.VMEM((n, stage, width), jnp.bfloat16),
            pltpu.VMEM((tdev, ta, 2 * tr), jnp.float32),
            pltpu.VMEM((tdev, ta, 2 * tr), jnp.bfloat16),
            pltpu.VMEM((ns, tdev, height, 2 * tr), jnp.bfloat16),
            pltpu.VMEM((tdev, 8, LANES), jnp.float32),
            pltpu.VMEM((ns, tdev, 8, LANES), jnp.float32),
            dma((3,)),
            dma((n, cap)),
            dma((n, cap)),
            dma((ns, tdev)),
            dma((ns, tdev)),
            dma((ns,)),
            dma((ns,)),
        ],
        compiler_params=pltpu.CompilerParams(
            collective_id=0, has_side_effects=True, vmem_limit_bytes=52 * 1024 * 1024
        ),
        cost_estimate=pl.CostEstimate(flops=5_000_000_000, bytes_accessed=14_000_000, transcendentals=0),
    )(send, azimuth[:, :, 0], range_interp)


def solution(mesh):
    in_specs = (
        P("tile", "subap", None, None, None),
        P("tile", "subap", None),
        P(),
        P("tile", None, "subap", None, None, None),
        P("tile", None, None, None),
    )
    out_specs = P("tile", None, "subap", None)
    return jax.shard_map(
        on_device, mesh=mesh, in_specs=in_specs, out_specs=out_specs, check_vma=False
    )
```

time: 236 us -> 86.1 us (0.36)
  Pallas kernels: 0 us -> 83.9 us
  blocking collectives: 76.6 us -> 0 us
  waiting for transfers between devices: 68.7 us -> 0 us
  local copies, waits for them, and re-layouts: 55 us -> 2.06 us
  other arithmetic: 13.5 us -> 0 us
  between operations: 13.5 us -> 0.03 us
  matrix products: 7.8 us -> 0 us
    pallas_call x0 -> x2, Pallas kernels: none -> 83.9 us  [the longest x1 75.4 us: on_device(): pl.pallas_call(functools.partial(kernel, dims), out_shape=jax.ShapeDtypeS...]
    all_to_all x1 -> x0, blocking collectives: 76.6 us -> none  [on_device(): lax.all_to_all(windows[:, None], 'tile', split_axis=0, concat_axis=1, til...]
    psum x1 -> x0, waiting for transfers between devices: 68.6 us -> none  [on_device(): raw = lax.psum(sub_image, 'subap')]
    unnamed x7, local copies, waits for them, and re-layouts: 21.2 us -> 2.06 us
    gather x1 -> x0, local copies, waits for them, and re-layouts: 17.7 us -> none  [cut(): return lax.dynamic_slice_in_dim(block, start, width, 2)]
    all_to_all x1 -> x0, local copies, waits for them, and re-layouts: 16.1 us -> none  [on_device(): lax.all_to_all(windows[:, None], 'tile', split_axis=0, concat_axis=1, til...]
    dot_general x2 -> x0, matrix products: 7.8 us -> none  [the longest x1 5.98 us: on_device(): jnp.einsum('tkcpr,tdru->tkcdpu', arrived, range_interp, preferred_element...]
    mul x1 -> x0, other arithmetic: 7.41 us -> none  [on_device(): windows = windows * hit[:, None, None, None]]
  transfers between devices with their start and end apart: 1 -> 0, of which waited for: 1 -> 0; matrix products, arithmetic and copies ran while one was open for 0% -> 0% of each run, Pallas kernels for 0% -> 0%
where the time goes in v1:
time: 86.1 us; the launch traced here: 86 us
  Pallas kernels  83.9 us (97%)
  local copies, waits for them, and re-layouts  2.06 us (2%)
    pallas_call x1, Pallas kernels, on_device(): pl.pallas_call(functools.partial(kernel, dims), out_shape=jax.ShapeDtypeS...  75.4 us
    pallas_call x1, Pallas kernels, on_device(): pl.pallas_call(functools.partial(cut_kernel, dims), grid=(n,), out_shape=...  8.51 us
    unnamed x7, local copies, waits for them, and re-layouts  2.06 us

profile of v1, /device:TPU:0, one launch (start us, length us, event | category | flops | bytes accessed | tf_op | source)
XLA Modules:
  0.0 86.0 jit_solution(5173301195648561792)
XLA Ops:
  0.0 0.0 copy-start
  0.0 0.7 copy-done
  0.7 0.0 copy-start.1
  0.7 0.7 copy-done.1
  1.3 0.0 copy-start.2
  1.3 8.5 %shard_map.55.send = bf16[8,528,512]{2,1,0:T(8,128)(2,1)} custom-call(s32[16]{0:T(128)S(1)} %bitcast.3, s32[24]{0:T(128)S(1)} %copy-done.1, bf16[256,16384]{1,0:T(8,128)(2,1)} %bitcast.4), custom_call_target="tpu_custom_call" | custom-call | flops 10000000 | bytes 13000000 | tf_op jit(solution)/shard_map/pallas_call | solution.py:210
  9.8 0.0 copy-done.2
  9.8 75.4 %shard_map.56 = f32[3,2,64,256]{3,2,1,0:T(8,128)S(1)} custom-call(bf16[8,528,512]{2,1,0:T(8,128)(2,1)} %shard_map.55.send, bf16[3,8,2,256,128]{4,3,2,1,0:T(8,128)(2,1)} %bitcast.5, bf16[3,2,512,256]{3,2,1,0:T(8,128)(2,1)S(1)} %copy-done.2), custom_call_target="tpu_custom_call" | custom-call | flops 5000000000 | bytes 14000000 | tf_op jit(solution)/shard_map/pallas_call | solution.py:220
  85.2 0.7 copy.7
Async XLA Ops:
  0.0 0.7 copy-start
  0.7 0.7 copy-start.1
  1.3 8.5 %copy-start.2 = (bf16[3,2,512,256]{3,2,1,0:T(8,128)(2,1)S(1)}, bf16[3,2,512,256]{3,2,1,0:T(8,128)(2,1)}, u32[]{:S(2)}) copy-start(bf16[3,2,512,256]{3,2,1,0:T(8,128)(2,1)} %interp.1) | copy-start | bytes 4718596

commit v2 on v1

--- a/solution.py
+++ b/solution.py
@@ -10,59 +10,14 @@
 MESH = pl.DeviceIdType.MESH
 LANES = 128
 FLAG_ROWS = 16
-CHUNK = 32
-
-
-def stage_at(slot, rows):
-    start = slot * rows + (FLAG_ROWS if slot > 0 else 0)
-    size = rows + (FLAG_ROWS if slot == 0 else 0)
-    return start, size
-
-
-def cut_kernel(dims, feet, offs, pulses, out, block, load_sem):
+
+
+def kernel(dims, info, pulses, azimuth, interp, out, block, az, table, send, recv, acc,
+           zsend, zrecv, psend, precv, load_sem, column_sem, send_sem, recv_sem, zsend_sem, zrecv_sem, psend_sem, precv_sem):
     n, ns, tdev, cap = dims
-    rows, reach = block.shape
-    width = out.shape[2]
-    slab = width + LANES
-    d = pl.program_id(0)
-    me = lax.axis_index("tile")
-    load = pltpu.make_async_copy(pulses, block, load_sem)
-
-    @pl.when(d == 0)
-    def _():
-        load.start()
-        load.wait()
-
-    lane = lax.broadcasted_iota(jnp.int32, (CHUNK, LANES), 1)
-    flag_row = lax.broadcasted_iota(jnp.int32, (FLAG_ROWS, width), 0)
-    owner = lax.rem(me + d, n)
-    first, second = feet[owner * cap], feet[owner * cap + 1]
-    low, high = jnp.minimum(first, second), jnp.maximum(first, second)
-    for slot in range(cap):
-        start = offs[high if slot else low]
-        base = jnp.minimum((start // LANES) * LANES, reach - slab)
-        base = pl.multiple_of(base, LANES)
-        shift = start - base
-        turn = lax.rem(LANES - shift + LANES, LANES)
-        keep = lane < LANES - shift
-        place = stage_at(slot, rows)[0]
-        for r in range(0, rows, CHUNK):
-            x = block[pl.ds(r, CHUNK), pl.ds(base, slab)].astype(jnp.float32)
-            turned = [
-                pltpu.roll(x[:, c * LANES:(c + 1) * LANES], turn, 1) for c in range(slab // LANES)
-            ]
-            y = [jnp.where(keep, turned[c], turned[c + 1]) for c in range(width // LANES)]
-            out[0, pl.ds(place + r, CHUNK)] = jnp.concatenate(y, axis=1).astype(jnp.bfloat16)
-    mine = owner * tdev
-    hit = (flag_row == low - mine) | (flag_row == tdev + high - mine)
-    out[0, pl.ds(rows, FLAG_ROWS)] = jnp.where(hit, 1.0, 0.0).astype(jnp.bfloat16)
-
-
-def kernel(dims, send, azimuth, interp, out, az, table, recv, acc,
-           zsend, zrecv, psend, precv, load_sem, send_sem, recv_sem, zsend_sem, zrecv_sem, psend_sem, precv_sem):
-    n, ns, tdev, cap = dims
-    half = az.shape[4]
-    rows = 2 * half
+    columns, rows = block.shape[:2]
+    half = rows // 2
+    width = recv.shape[2]
     ta, two_tr = acc.shape[1:]
     tr = two_tr // 2
     height = ta // ns
@@ -71,8 +26,23 @@
 
     loads = [
         pltpu.make_async_copy(src, dst, load_sem.at[i])
-        for i, (src, dst) in enumerate(((send.at[0], recv.at[0]), (interp, table), (azimuth, az)))
+        for i, (src, dst) in enumerate(((interp, table), (azimuth, az)))
     ]
+
+    def column_copy(c):
+        return pltpu.make_async_copy(
+            pulses.at[:, pl.ds(pl.multiple_of(c * LANES, LANES), LANES)], block.at[c], column_sem.at[c]
+        )
+
+    def fetch(c, carry):
+        column_copy(c).start()
+        return carry
+
+    def fetched(c, carry):
+        column_copy(c).wait()
+        return carry
+
+    lax.fori_loop(0, columns, fetch, 0)
     for load in loads:
         load.start()
 
@@ -82,8 +52,13 @@
     for e in range(1, ns):
         pl.semaphore_signal(barrier, inc=1, device_id={"subap": lax.rem(mz + e, ns)}, device_id_type=MESH)
 
+    def at(slot):
+        start = slot * rows + (FLAG_ROWS if slot > 0 else 0)
+        size = rows + (FLAG_ROWS if slot == 0 else 0)
+        return start, size
+
     def window_copy(d, slot):
-        start, size = stage_at(slot, rows)
+        start, size = at(slot)
         return pltpu.make_async_remote_copy(
             src_ref=send.at[d, pl.ds(start, size)],
             dst_ref=recv.at[d, pl.ds(start, size)],
@@ -93,12 +68,37 @@
             device_id_type=MESH,
         )
 
+    taken = lax.broadcasted_iota(jnp.int32, (2 * LANES, LANES), 0) - lax.broadcasted_iota(
+        jnp.int32, (2 * LANES, LANES), 1
+    )
+    flag_row = lax.broadcasted_iota(jnp.int32, (FLAG_ROWS, width), 0)
+
+    def cut(d, slot):
+        owner = lax.rem(me + d, n)
+        entry = owner * cap + slot
+        base, shift = info[entry], info[n * cap + entry]
+        pick = jnp.where(taken == shift, 1.0, 0.0).astype(jnp.bfloat16)
+        place = at(slot)[0]
+        x = [block[base + c] for c in range(width // LANES + 1)]
+        for c in range(width // LANES):
+            pair = jnp.concatenate(x[c:c + 2], axis=1)
+            y = jnp.dot(pair, pick, preferred_element_type=jnp.float32)
+            send[d, pl.ds(place, rows), c * LANES:(c + 1) * LANES] = y.astype(jnp.bfloat16)
+        if slot == 0:
+            low, high = info[2 * n * cap + entry], info[2 * n * cap + entry + 1]
+            hit = (flag_row == low) | (flag_row == tdev + high)
+            send[d, pl.ds(rows, FLAG_ROWS)] = jnp.where(hit, 1.0, 0.0).astype(jnp.bfloat16)
+
+    lax.fori_loop(0, columns, fetched, 0)
     pl.semaphore_wait(barrier, n + ns - 2)
     for slot in range(cap):
         def issue(i, carry, slot=slot):
+            cut(n - i, slot)
             window_copy(n - i, slot).start()
             return carry
         lax.fori_loop(1, n, issue, 0)
+    for slot in range(cap):
+        cut(0, slot)
     for load in loads:
         load.wait()
 
@@ -108,7 +108,7 @@
         for slot in range(cap):
             if slot <= t <= tdev - cap + slot:
                 row = slot * tdev + t
-                term = buf[d, pl.ds(stage_at(slot, rows)[0], rows)] * flags[row:row + 1].astype(jnp.bfloat16)
+                term = buf[d, pl.ds(at(slot)[0], rows)] * flags[row:row + 1].astype(jnp.bfloat16)
                 w = term if w is None else w + term
         pr = jnp.dot(w, table[t, 0], preferred_element_type=jnp.float32)
         pi = jnp.dot(w, table[t, 1], preferred_element_type=jnp.float32)
@@ -133,7 +133,7 @@
         )
 
     for t in range(tdev):
-        acc[t] = add(recv, 0, t)
+        acc[t] = add(send, 0, t)
     for slot in range(cap):
         done = [t for t in range(tdev) if min(t, cap - 1) == slot]
 
@@ -203,35 +203,36 @@
     ta = azimuth.shape[4]
     height = ta // ns
     stage = cap * rows + FLAG_ROWS
+    columns = pulses.shape[4] // LANES
+    feet = footprint.reshape(n, cap)
+    low, high = jnp.min(feet, axis=1), jnp.max(feet, axis=1)
+    tiles = jnp.stack([low, high], axis=1).reshape(-1)
+    ids = jnp.arange(offsets.shape[0], dtype=jnp.int32)
+    start = jnp.sum(jnp.where(tiles[:, None] == ids[None], offsets[None], 0), axis=1)
+    base = jnp.minimum(start // LANES, columns - width // LANES - 1)
+    local = tiles - jnp.repeat(jnp.arange(n, dtype=jnp.int32), cap) * tdev
+    info = jnp.concatenate([base, start - base * LANES, local])
     dma = pltpu.SemaphoreType.DMA
     smem = pl.BlockSpec(memory_space=pltpu.SMEM)
     hbm = pl.BlockSpec(memory_space=pl.ANY)
-    dims = (n, ns, tdev, cap)
-    send = pl.pallas_call(
-        functools.partial(cut_kernel, dims),
-        grid=(n,),
-        out_shape=jax.ShapeDtypeStruct((n, stage, width), jnp.bfloat16),
-        in_specs=[smem, smem, hbm],
-        out_specs=pl.BlockSpec((1, stage, width), lambda d: (d, 0, 0)),
-        scratch_shapes=[pltpu.VMEM((rows, pulses.shape[4]), jnp.bfloat16), dma],
-        compiler_params=pltpu.CompilerParams(vmem_limit_bytes=52 * 1024 * 1024),
-        cost_estimate=pl.CostEstimate(flops=10_000_000, bytes_accessed=13_000_000, transcendentals=0),
-    )(footprint.reshape(-1), offsets, pulses.reshape(rows, pulses.shape[4]))
     return pl.pallas_call(
-        functools.partial(kernel, dims),
+        functools.partial(kernel, (n, ns, tdev, cap)),
         out_shape=jax.ShapeDtypeStruct((tdev, 2, height, tr), jnp.float32),
-        in_specs=[hbm, hbm, hbm],
+        in_specs=[smem, hbm, hbm, hbm],
         out_specs=pl.BlockSpec(memory_space=pltpu.VMEM),
         scratch_shapes=[
+            pltpu.VMEM((columns, rows, LANES), jnp.bfloat16),
             pltpu.VMEM((tdev, n, 2, ta, rows // 2), jnp.bfloat16),
             pltpu.VMEM((tdev, 2, width, tr), jnp.bfloat16),
+            pltpu.VMEM((n, stage, width), jnp.bfloat16),
             pltpu.VMEM((n, stage, width), jnp.bfloat16),
             pltpu.VMEM((tdev, ta, 2 * tr), jnp.float32),
             pltpu.VMEM((tdev, ta, 2 * tr), jnp.bfloat16),
             pltpu.VMEM((ns, tdev, height, 2 * tr), jnp.bfloat16),
             pltpu.VMEM((tdev, 8, LANES), jnp.float32),
             pltpu.VMEM((ns, tdev, 8, LANES), jnp.float32),
-            dma((3,)),
+            dma((2,)),
+            dma((columns,)),
             dma((n, cap)),
             dma((n, cap)),
             dma((ns, tdev)),
@@ -243,7 +244,7 @@
             collective_id=0, has_side_effects=True, vmem_limit_bytes=52 * 1024 * 1024
         ),
         cost_estimate=pl.CostEstimate(flops=5_000_000_000, bytes_accessed=14_000_000, transcendentals=0),
-    )(send, azimuth[:, :, 0], range_interp)
+    )(info, pulses.reshape(rows, pulses.shape[4]), azimuth[:, :, 0], range_interp)
 
 
 def solution(mesh):

time: 86.1 us -> 84.8 us (0.985)
  Pallas kernels: 83.9 us -> 79.2 us
  other arithmetic: 0 us -> 2.43 us
  local copies, waits for them, and re-layouts: 2.06 us -> 2.99 us
    pallas_call x2 -> x1, Pallas kernels: 83.9 us -> 79.2 us  [on_device(): pl.pallas_call(functools.partial(kernel, (n, ns, tdev, cap)), out_shape=j...]
    unnamed x0 -> x1, other arithmetic: none -> 1.32 us
    unnamed x7 -> x4, local copies, waits for them, and re-layouts: 2.06 us -> 2.67 us
where the time goes in v2:
time: 84.8 us; the launch traced here: 84.6 us
  Pallas kernels  79.2 us (93%)
  local copies, waits for them, and re-layouts  2.99 us (4%)
  other arithmetic  2.43 us (3%)
    pallas_call x1, Pallas kernels, on_device(): pl.pallas_call(functools.partial(kernel, (n, ns, tdev, cap)), out_shape=j...  79.2 us
    unnamed x4, local copies, waits for them, and re-layouts  2.67 us

profile of v2, /device:TPU:0, one launch (start us, length us, event | category | flops | bytes accessed | tf_op | source)
XLA Modules:
  0.0 84.6 jit_solution(7078954318744702986)
XLA Ops:
  0.0 0.5 broadcast.30
  0.5 1.3 %reduce.3 = s32[16]{0:T(128)S(1)} reduce(s32[1,1,16]{2,1,0:T(1,128)} %param.6, s32[]{:T(128)} %broadcast.30), dimensions={0,1}, to_apply=%param.6.reduce_sub_computation.3 | reduce | bytes 132 | tf_op args[1]
  1.8 0.1 reshape.12
  1.9 0.2 fusion.1
  2.1 0.1 copy.8
  2.2 0.1 eq.15
  2.2 0.8 select_reduce_fusion
  3.1 0.1 mul.11
  3.2 0.1 pad_add_fusion.1.info
  3.3 0.0 copy-start
  3.3 1.4 %copy-done = bf16[3,2,512,256]{3,2,1,0:T(8,128)(2,1)S(1)} copy-done((bf16[3,2,512,256]{3,2,1,0:T(8,128)(2,1)S(1)}, bf16[3,2,512,256]{3,2,1,0:T(8,128)(2,1)}, u32[]{:S(2)}) %copy-start) | copy-done | bytes 1572888
  4.7 79.2 %shard_map.55 = f32[3,2,64,256]{3,2,1,0:T(8,128)S(1)} custom-call(s32[48]{0:T(128)S(1)} %pad_add_fusion.1.info, bf16[256,16384]{1,0:T(8,128)(2,1)} %bitcast.6, bf16[3,8,2,256,128]{4,3,2,1,0:T(8,128)(2,1)} %bitcast.7, bf16[3,2,512,256]{3,2,1,0:T(8,128)(2,1)S(1)} %copy-done), custom_call_target="tpu_custom_call" | custom-call | flops 5000000000 | bytes 14000000 | tf_op jit(solution)/shard_map/pallas_call | solution.py:218
  83.9 0.7 copy.10
  (4 shorter events, 0.0 us)
Async XLA Ops:
  3.3 1.4 %copy-start = (bf16[3,2,512,256]{3,2,1,0:T(8,128)(2,1)S(1)}, bf16[3,2,512,256]{3,2,1,0:T(8,128)(2,1)}, u32[]{:S(2)}) copy-start(bf16[3,2,512,256]{3,2,1,0:T(8,128)(2,1)} %interp.1) | copy-start | bytes 4718596

commit v3 on v2

--- a/solution.py
+++ b/solution.py
@@ -10,6 +10,20 @@
 MESH = pl.DeviceIdType.MESH
 LANES = 128
 FLAG_ROWS = 16
+
+
+def plan_kernel(dims, last, feet, offs, info):
+    n, tdev, cap = dims
+    for owner in range(n):
+        first, second = feet[owner * cap], feet[owner * cap + 1]
+        for slot in range(cap):
+            entry = owner * cap + slot
+            tile = jnp.maximum(first, second) if slot else jnp.minimum(first, second)
+            start = offs[tile]
+            base = jnp.minimum(lax.div(start, LANES), last)
+            info[entry] = base
+            info[n * cap + entry] = start - base * LANES
+            info[2 * n * cap + entry] = tile - owner * tdev
 
 
 def kernel(dims, info, pulses, azimuth, interp, out, block, az, table, send, recv, acc,
@@ -94,7 +108,8 @@
     for slot in range(cap):
         def issue(i, carry, slot=slot):
             cut(n - i, slot)
-            window_copy(n - i, slot).start()
+            if slot == 0:
+                window_copy(n - i, slot).start()
             return carry
         lax.fori_loop(1, n, issue, 0)
     for slot in range(cap):
@@ -135,6 +150,12 @@
     for t in range(tdev):
         acc[t] = add(send, 0, t)
     for slot in range(cap):
+        if slot + 1 < cap:
+            def follow(i, carry, slot=slot):
+                window_copy(n - i, slot).wait_send()
+                window_copy(n - i, slot + 1).start()
+                return carry
+            lax.fori_loop(1, n, follow, 0)
         done = [t for t in range(tdev) if min(t, cap - 1) == slot]
 
         def gather(d, carry, slot=slot, done=done):
@@ -183,11 +204,10 @@
         out[t, 0] = x[:, :tr]
         out[t, 1] = x[:, tr:]
 
-    for slot in range(cap):
-        def drain(d, carry, slot=slot):
-            window_copy(d, slot).wait_send()
-            return carry
-        lax.fori_loop(1, n, drain, 0)
+    def drain(d, carry):
+        window_copy(d, cap - 1).wait_send()
+        return carry
+    lax.fori_loop(1, n, drain, 0)
     for e in range(1, ns):
         power_copy(e).wait_send()
         for t in range(tdev):
@@ -204,17 +224,15 @@
     height = ta // ns
     stage = cap * rows + FLAG_ROWS
     columns = pulses.shape[4] // LANES
-    feet = footprint.reshape(n, cap)
-    low, high = jnp.min(feet, axis=1), jnp.max(feet, axis=1)
-    tiles = jnp.stack([low, high], axis=1).reshape(-1)
-    ids = jnp.arange(offsets.shape[0], dtype=jnp.int32)
-    start = jnp.sum(jnp.where(tiles[:, None] == ids[None], offsets[None], 0), axis=1)
-    base = jnp.minimum(start // LANES, columns - width // LANES - 1)
-    local = tiles - jnp.repeat(jnp.arange(n, dtype=jnp.int32), cap) * tdev
-    info = jnp.concatenate([base, start - base * LANES, local])
     dma = pltpu.SemaphoreType.DMA
     smem = pl.BlockSpec(memory_space=pltpu.SMEM)
     hbm = pl.BlockSpec(memory_space=pl.ANY)
+    info = pl.pallas_call(
+        functools.partial(plan_kernel, (n, tdev, cap), columns - width // LANES - 1),
+        out_shape=jax.ShapeDtypeStruct((3 * n * cap,), jnp.int32),
+        in_specs=[smem, smem],
+        out_specs=smem,
+    )(footprint.reshape(-1), offsets)
     return pl.pallas_call(
         functools.partial(kernel, (n, ns, tdev, cap)),
         out_shape=jax.ShapeDtypeStruct((tdev, 2, height, tr), jnp.float32),
@@ -241,7 +259,7 @@
             dma((ns,)),
         ],
         compiler_params=pltpu.CompilerParams(
-            collective_id=0, has_side_effects=True, vmem_limit_bytes=52 * 1024 * 1024
+            collective_id=0, has_side_effects=True, vmem_limit_bytes=62 * 1024 * 1024
         ),
         cost_estimate=pl.CostEstimate(flops=5_000_000_000, bytes_accessed=14_000_000, transcendentals=0),
     )(info, pulses.reshape(rows, pulses.shape[4]), azimuth[:, :, 0], range_interp)

time: 84.8 us -> 83.4 us (0.983)
  other arithmetic: 2.43 us -> 0 us
  Pallas kernels: 79.2 us -> 81.4 us
  local copies, waits for them, and re-layouts: 2.99 us -> 1.78 us
    unnamed x1 -> x0, other arithmetic: 1.32 us -> none
    pallas_call x0 -> x1, Pallas kernels: none -> 1.27 us  [on_device(): pl.pallas_call(functools.partial(plan_kernel, (n, tdev, cap), columns - w...]
    pallas_call x1, Pallas kernels: 79.2 us -> 80.1 us  [on_device(): pl.pallas_call(functools.partial(kernel, (n, ns, tdev, cap)), out_shape=j...]
    unnamed x4 -> x1, local copies, waits for them, and re-layouts: 2.67 us -> 1.78 us
where the time goes in v3:
time: 83.4 us; the launch traced here: 83.2 us
  Pallas kernels  81.4 us (98%)
  local copies, waits for them, and re-layouts  1.78 us (2%)
    pallas_call x1, Pallas kernels, on_device(): pl.pallas_call(functools.partial(kernel, (n, ns, tdev, cap)), out_shape=j...  80.1 us
    unnamed x1, local copies, waits for them, and re-layouts  1.78 us

profile of v3, /device:TPU:0, one launch (start us, length us, event | category | flops | bytes accessed | tf_op | source)
XLA Modules:
  0.0 83.2 jit_solution(6048235159428295848)
XLA Ops:
  0.0 1.3 %shard_map.55.info = s32[48]{0:T(128)} custom-call(s32[16]{0:T(128)} %bitcast.5, s32[24]{0:T(128)} %offs.1), custom_call_target="tpu_custom_call" | custom-call | tf_op jit(solution)/shard_map/pallas_call | solution.py:230
  1.3 80.1 %shard_map.56 = f32[3,2,64,256]{3,2,1,0:T(8,128)} custom-call(s32[48]{0:T(128)} %shard_map.55.info, bf16[256,16384]{1,0:T(8,128)(2,1)} %bitcast.3, bf16[3,8,2,256,128]{4,3,2,1,0:T(8,128)(2,1)} %bitcast.4, bf16[3,2,512,256]{3,2,1,0:T(8,128)(2,1)} %interp.1), custom_call_target="tpu_custom_call" | custom-call | flops 5000000000 | bytes 14000000 | tf_op jit(solution)/shard_map/pallas_call | solution.py:236
  81.4 1.8 %copy.7 = f32[3,2,64,256]{3,2,1,0:T(8,128)} copy(f32[3,2,64,256]{3,2,1,0:T(8,128)} %shard_map.56) | data formatting | bytes 786432

commit v4 on v3

--- a/solution.py
+++ b/solution.py
@@ -158,13 +158,13 @@
             lax.fori_loop(1, n, follow, 0)
         done = [t for t in range(tdev) if min(t, cap - 1) == slot]
 
-        def gather(d, carry, slot=slot, done=done):
-            window_copy(d, slot).wait_recv()
-            for t in done:
+        for t in done:
+            def gather(d, carry, slot=slot, t=t, first=t == done[0]):
+                if first:
+                    window_copy(d, slot).wait_recv()
                 acc[t] += add(recv, d, t)
-            return carry
-        lax.fori_loop(1, n, gather, 0)
-        for t in done:
+                return carry
+            lax.fori_loop(1, n, gather, 0)
             zsend[t] = acc[t].astype(jnp.bfloat16)
             for e in range(1, ns):
                 image_copy(e, t).start()

time: 83.4 us -> 80.4 us (0.964)
  Pallas kernels: 81.4 us -> 78.5 us
    pallas_call x1, Pallas kernels: 80.1 us -> 77.2 us  [on_device(): pl.pallas_call(functools.partial(kernel, (n, ns, tdev, cap)), out_shape=j...]
where the time goes in v4:
time: 80.4 us; the launch traced here: 80.3 us
  Pallas kernels  78.5 us (98%)
  local copies, waits for them, and re-layouts  1.78 us (2%)
    pallas_call x1, Pallas kernels, on_device(): pl.pallas_call(functools.partial(kernel, (n, ns, tdev, cap)), out_shape=j...  77.2 us
    unnamed x1, local copies, waits for them, and re-layouts  1.78 us

profile of v4, /device:TPU:0, one launch (start us, length us, event | category | flops | bytes accessed | tf_op | source)
XLA Modules:
  0.0 80.3 jit_solution(17424051512005712152)
XLA Ops:
  0.0 1.3 %shard_map.55.info = s32[48]{0:T(128)} custom-call(s32[16]{0:T(128)} %bitcast.5, s32[24]{0:T(128)} %offs.1), custom_call_target="tpu_custom_call" | custom-call | tf_op jit(solution)/shard_map/pallas_call | solution.py:230
  1.3 77.2 %shard_map.56 = f32[3,2,64,256]{3,2,1,0:T(8,128)} custom-call(s32[48]{0:T(128)} %shard_map.55.info, bf16[256,16384]{1,0:T(8,128)(2,1)} %bitcast.3, bf16[3,8,2,256,128]{4,3,2,1,0:T(8,128)(2,1)} %bitcast.4, bf16[3,2,512,256]{3,2,1,0:T(8,128)(2,1)} %interp.1), custom_call_target="tpu_custom_call" | custom-call | flops 5000000000 | bytes 14000000 | tf_op jit(solution)/shard_map/pallas_call | solution.py:236
  78.5 1.8 %copy.7 = f32[3,2,64,256]{3,2,1,0:T(8,128)} copy(f32[3,2,64,256]{3,2,1,0:T(8,128)} %shard_map.56) | data formatting | bytes 786432

commit v5 on v4

--- a/solution.py
+++ b/solution.py
@@ -159,7 +159,8 @@
         done = [t for t in range(tdev) if min(t, cap - 1) == slot]
 
         for t in done:
-            def gather(d, carry, slot=slot, t=t, first=t == done[0]):
+            def gather(i, carry, slot=slot, t=t, first=t == done[0]):
+                d = n - i
                 if first:
                     window_copy(d, slot).wait_recv()
                 acc[t] += add(recv, d, t)

time: 80.4 us -> 78.9 us (0.981)
  Pallas kernels: 78.5 us -> 76.9 us
    pallas_call x1, Pallas kernels: 77.2 us -> 75.6 us  [on_device(): pl.pallas_call(functools.partial(kernel, (n, ns, tdev, cap)), out_shape=j...]
where the time goes in v5:
time: 78.9 us; the launch traced here: 78.7 us
  Pallas kernels  76.9 us (97%)
  local copies, waits for them, and re-layouts  1.78 us (2%)
    pallas_call x1, Pallas kernels, on_device(): pl.pallas_call(functools.partial(kernel, (n, ns, tdev, cap)), out_shape=j...  75.6 us
    unnamed x1, local copies, waits for them, and re-layouts  1.78 us

profile of v5, /device:TPU:0, one launch (start us, length us, event | category | flops | bytes accessed | tf_op | source)
XLA Modules:
  0.0 78.7 jit_solution(7147493728941213920)
XLA Ops:
  0.0 1.3 %shard_map.55.info = s32[48]{0:T(128)} custom-call(s32[16]{0:T(128)} %bitcast.5, s32[24]{0:T(128)} %offs.1), custom_call_target="tpu_custom_call" | custom-call | tf_op jit(solution)/shard_map/pallas_call | solution.py:231
  1.3 75.6 %shard_map.56 = f32[3,2,64,256]{3,2,1,0:T(8,128)} custom-call(s32[48]{0:T(128)} %shard_map.55.info, bf16[256,16384]{1,0:T(8,128)(2,1)} %bitcast.3, bf16[3,8,2,256,128]{4,3,2,1,0:T(8,128)(2,1)} %bitcast.4, bf16[3,2,512,256]{3,2,1,0:T(8,128)(2,1)} %interp.1), custom_call_target="tpu_custom_call" | custom-call | flops 5000000000 | bytes 14000000 | tf_op jit(solution)/shard_map/pallas_call | solution.py:237
  76.9 1.8 %copy.7 = f32[3,2,64,256]{3,2,1,0:T(8,128)} copy(f32[3,2,64,256]{3,2,1,0:T(8,128)} %shard_map.56) | data formatting | bytes 786432
